TPU v7x, 32 devices: a whole 2x2x4 slice. The times are simulated.
32 devices in a mesh: dp: 4 (over y, core), expert: 8 (over z, x).
Axes of the slice: x: 2, y: 2, z: 4, core: 2. Of those that a mesh axis runs over, the one named last changes fastest.
Arguments:
- tokens: bfloat16 [2048, 2048], P(('dp', 'expert')), may hold values from -6 to 6
- expert_ids: int32 [2048, 8], P(('dp', 'expert')), may hold values from 0 to 15, as said below
- gates: bfloat16 [2048, 8], P(('dp', 'expert')), may hold values from 0.049804688 to 0.59765625
- kept_token: int32 [4, 16, 384], P('dp', 'expert'), may hold values from 0 to 511, as said below
- kept_count: int32 [4, 16, 8], P('dp', 'expert'), may hold values from 0 to 48, as said below
- w_gate: bfloat16 [16, 2048, 768], P('expert', 'dp'), may hold values from -0.125 to 0.125
- w_up: bfloat16 [16, 2048, 768], P('expert', 'dp'), may hold values from -0.125 to 0.125
- w_down: bfloat16 [16, 768, 2048], P('expert', None, 'dp'), may hold values from -0.21875 to 0.21875
Outputs:
- moe_output: bfloat16 [2048, 2048], P(('dp', 'expert'))
Inputs may be any that keep to these rules, and one draw needn't show every extreme that they name: `expert_ids`: each row names 8 different experts. `kept_token`: slots c * 48 to c * 48 + 47 of expert e hold tokens of source device c of the group (tokens c * 64 to c * 64 + 63). The first kept_count[a, e, c] of them are, in rising order, the first tokens of that device whose expert_ids row names e; the other slots hold arbitrary tokens of that device. kept_count[a, e, c] is the number of tokens of source device c naming e, capped at 48. In every data group some expert has all its counts equal to 48.
All inputs are finite; a program needn't handle non-finite values.
Results may differ from a plain program's by a relative error of at most 0.005.
Values may be sent and summed in bfloat16 or wider, within the bound.
A program may use at most 128 MiB of HBM per device.

v0:
```python
import jax
import jax.numpy as jnp
from jax import lax
from jax.sharding import PartitionSpec as P


def expert_ffn(token_rows, w_gate, w_up, w_down):
    gate_new = jnp.einsum(
        "ecd,edf->ecf",
        token_rows,
        lax.all_gather(w_gate, "dp", axis=1, tiled=True),
        preferred_element_type=jnp.float32,
    )
    up_new = jnp.einsum(
        "ecd,edf->ecf",
        token_rows,
        lax.all_gather(w_up, "dp", axis=1, tiled=True),
        preferred_element_type=jnp.float32,
    )
    hidden = (jax.nn.silu(gate_new) * up_new).astype(jnp.bfloat16)
    return jnp.einsum(
        "ecf,efd->ecd",
        hidden,
        lax.all_gather(w_down, "dp", axis=2, tiled=True),
        preferred_element_type=jnp.float32,
    )


def body(tokens, expert_ids, gates, kept_token, kept_count, w_gate, w_up, w_down):
    my_rank = lax.axis_index("expert")
    peers = lax.axis_size("expert")
    per_device = w_gate.shape[0]
    tok_dev = tokens.shape[0]
    width = tokens.shape[1]
    top_count = expert_ids.shape[1]
    slot_list = kept_token[0]
    counts = kept_count[0]
    cap_e = slot_list.shape[1]
    cap_src = cap_e // peers
    group_size = tok_dev * peers
    mine = my_rank * per_device + jnp.arange(per_device, dtype=jnp.int32)
    usable = (jnp.arange(cap_e, dtype=jnp.int32) % cap_src)[None, :] < jnp.repeat(
        counts, cap_src, axis=1
    )
    start_bufs = (
        jnp.zeros((group_size, width), jnp.bfloat16),
        jnp.zeros((group_size, top_count), jnp.int32),
        jnp.zeros((group_size, top_count), jnp.bfloat16),
    )
    pieces = (
        lax.all_gather(tokens, "expert", axis=0, tiled=True),
        lax.all_gather(expert_ids, "expert", axis=0, tiled=True),
        lax.all_gather(gates, "expert", axis=0, tiled=True),
    )
    first_row = jnp.int32(0)
    group_rows, group_ids, group_gates = tuple(
        (lax.dynamic_update_slice_in_dim(start_bufs[i], pieces[i], first_row, 0) for i in range(3))
    )
    token_rows = group_rows[slot_list]
    names_it = group_ids[slot_list] == mine[:, None, None]
    slot_weight = jnp.sum(
        jnp.where(names_it, group_gates[slot_list].astype(jnp.float32), 0.0), axis=2
    )
    slot_weight = jnp.where(usable, slot_weight, 0.0)
    outputs = expert_ffn(token_rows, w_gate, w_up, w_down)
    flat_out = (outputs * slot_weight[:, :, None]).reshape(-1, width)
    summed_all = jnp.zeros((group_size, width), jnp.float32).at[slot_list.reshape(-1)].add(flat_out)
    return lax.psum_scatter(summed_all, "expert", scatter_dimension=0, tiled=True).astype(
        jnp.bfloat16
    )


def solution(mesh):
    return jax.shard_map(
        body,
        mesh=mesh,
        in_specs=(
            P(("dp", "expert"), None),
            P(("dp", "expert"), None),
            P(("dp", "expert"), None),
            P("dp", "expert", None),
            P("dp", "expert", None),
            P("expert", "dp", None),
            P("expert", "dp", None),
            P("expert", None, "dp"),
        ),
        out_specs=P(("dp", "expert"), None),
        check_vma=False,
    )
```

profile of v0, /device:TPU:0, one launch (start us, length us, event | category | flops | bytes accessed | tf_op | source)
XLA Modules:
  0.0 330.6 jit_solution(17146731000908118260)
XLA Ops:
  6.5 0.0 copy-start
  6.5 0.0 copy-start.1
  6.5 0.0 copy-start.2
  6.5 0.0 all-gather.7.cloned.1.call-start
  6.5 0.7 all-gather.7.cloned.1.call-update
  7.3 0.0 all-gather.9.cloned.1.call-start
  7.3 0.7 all-gather.9.cloned.1.call-update
  8.0 0.0 all-gather.11.cloned.1.call-start
  8.1 0.7 all-gather.11.cloned.1.call-update
  8.7 0.0 all-gather.13.cloned.1.call-start
  8.8 0.5 all-gather.13.cloned.1.call-update
  9.3 0.0 copy-start.3
  9.3 0.0 reduce-scatter.2.cloned.1.call-start
  9.4 0.0 copy-done
  9.4 0.0 copy-done.1
  9.4 32.5 %all-gather = s32[8,64,8]{1,2,0:T(8,128)S(1)} all-gather(s32[1,64,8]{1,2,0:T(8,128)S(1)} %bitcast.30), channel_id=1, replica_groups=mesh['dp'=4,'expert'=8] {'expert'}, dimensions={0}, use_global_device_ids=true | all-gather | bytes 18432 | tf_op jit(solution)/shard_map/all_gather | solution.py:52
  42.0 0.1 copy.13
  42.1 0.0 copy-done.2
  42.1 26.2 %all-gather.1 = bf16[8,64,8]{1,2,0:T(8,128)(2,1)S(1)} all-gather(bf16[1,64,8]{1,2,0:T(8,128)(2,1)S(1)} %bitcast.31), channel_id=1, replica_groups=mesh['dp'=4,'expert'=8] {'expert'}, dimensions={0}, use_global_device_ids=true | all-gather | bytes 9216 | tf_op jit(solution)/shard_map/all_gather | solution.py:53
  68.3 0.1 copy.14
  68.4 1.6 gather_fusion.1
  70.0 1.9 gather_fusion.2
  71.9 0.0 copy-done.3
  71.9 0.1 broadcast_in_dim.22
  71.9 0.1 reshape.95
  72.1 0.2 fusion.3
  72.3 0.0 all-gather.7.cloned.1.call-done
  72.3 8.4 %gather_fusion = bf16[768,2048]{1,0:T(8,128)(2,1)S(1)} fusion(bf16[512,2048]{1,0:T(8,128)(2,1)} %all-gather.7.cloned.1.call-done, s32[1024]{0:T(1024)S(1)} %pad_clamp_fusion), kind=kCustom, calls=%fused_computation | custom fusion | bytes 6294528 | tf_op jit(solution)/shard_map/gather | solution.py:59
  80.7 27.6 %all-gather.9.cloned.1.call-done = bf16[2,2048,768]{2,1,0:T(8,128)(2,1)} async-done(((bf16[2,512,768]{2,1,0:T(8,128)(2,1)}), bf16[2,2048,768]{2,1,0:T(8,128)(2,1)}) %all-gather.9.cloned.1.call-update) | async-done | bytes 6291472 | tf_op jit(solution)/shard_map/all_gather | solution.py:11
  108.3 6.8 %fusion.9 = f32[2,384,768]{2,1,0:T(8,128)} fusion(bf16[2,384,2048]{2,1,0:T(8,128)(2,1)S(1)} %bitcast.24, bf16[2,2048,768]{2,1,0:T(8,128)(2,1)} %all-gather.9.cloned.1.call-done), kind=kOutput, calls=%fused_computation.23 | convolution fusion | flops 2415919104 | bytes 11796480 | tf_op jit(solution)/shard_map/ecd,edf->ecf/dot_general | solution.py:8
  115.0 41.2 %all-gather.11.cloned.1.call-done = bf16[2,2048,768]{2,1,0:T(8,128)(2,1)} async-done(((bf16[2,512,768]{2,1,0:T(8,128)(2,1)}), bf16[2,2048,768]{2,1,0:T(8,128)(2,1)}) %all-gather.11.cloned.1.call-update) | async-done | bytes 6291472 | tf_op jit(solution)/shard_map/all_gather | solution.py:17
  156.3 47.8 %all-gather.13.cloned.1.call-done = bf16[2,768,2048]{2,1,0:T(8,128)(2,1)} async-done(((bf16[2,768,512]{2,1,0:T(8,128)(2,1)}), bf16[2,768,2048]{2,1,0:T(8,128)(2,1)}) %all-gather.13.cloned.1.call-update) | async-done | bytes 6291472 | tf_op jit(solution)/shard_map/all_gather | solution.py:24
  204.1 13.1 %convolution_multiply_fusion = f32[2,384,2048]{2,1,0:T(8,128)} fusion(bf16[2,768,2048]{2,1,0:T(8,128)(2,1)} %all-gather.13.cloned.1.call-done, f32[2,384]{1,0:T(2,128)S(1)} %compare_select_fusion.2, f32[2,384,768]{2,1,0:T(8,128)} %fusion.9, bf16[2,384,2048]{2,1,0:T(8,128)(2,1)S(1)} %bitcast.25, bf16[2,2048,768]{2,1,0:T(8,128)(2,1)} %all-gather.11.cloned.1.call-done), kind=kOutput, calls=%fused_computation.4 | convolution fusion | flops 4836950016 | bytes 24382464 | tf_op jit(solution)/shard_map/ecf,efd->ecd/dot_general | solution.py:21
  217.1 17.0 %scatter_custom_fusion = f32[512,2048]{1,0:T(8,128)} fusion(s32[768]{0:T(1024)S(1)} %fusion.4, f32[768,2048]{1,0:T(8,128)} %bitcast.33, f32[]{:T(128)} %constant.8.clone.1), kind=kCustom, calls=%fused_computation.6 | custom fusion | flops 1572864 | bytes 4194816 | tf_op jit(solution)/shard_map/scatter-add | solution.py:67
  234.2 0.0 reduce-scatter.2.cloned.1.call-update
  234.2 88.1 %reduce-scatter.2.cloned.1.call-done = f32[64,2048]{1,0:T(8,128)} async-done(((f32[512,2048]{1,0:T(8,128)}), f32[64,2048]{1,0:T(8,128)}) %reduce-scatter.2.cloned.1.call-update) | async-done | bytes 524304 | tf_op jit(solution)/shard_map/reduce_scatter | solution.py:68
  322.3 1.8 convert_element_type.11
  (8 shorter events, 0.1 us)
Async XLA Ops:
  6.5 2.9 copy-start
  6.5 2.9 copy-start.1
  6.5 35.6 %copy-start.2 = (bf16[64,8]{0,1:T(8,128)(2,1)S(1)}, bf16[64,8]{0,1:T(8,128)(2,1)}, u32[]{:S(2)}) copy-start(bf16[64,8]{0,1:T(8,128)(2,1)} %param.10) | copy-start | bytes 3076
  6.5 65.8 %all-gather.7.cloned.1.call-start = ((), (), s32[]{:S(2)}) async-start(), calls=%async_computation.1 | async-start | bytes 2359296 | tf_op jit(solution)/shard_map/all_gather | solution.py:51
  7.3 101.0 %all-gather.9.cloned.1.call-start = ((), (), s32[]{:S(2)}) async-start(), calls=%async_computation.2 | async-start | bytes 7864320 | tf_op jit(solution)/shard_map/all_gather | solution.py:11
  8.0 148.2 %all-gather.11.cloned.1.call-start = ((), (), s32[]{:S(2)}) async-start(), calls=%async_computation.3 | async-start | bytes 7864320 | tf_op jit(solution)/shard_map/all_gather | solution.py:17
  8.7 195.3 %all-gather.13.cloned.1.call-start = ((), (), s32[]{:S(2)}) async-start(), calls=%async_computation.4 | async-start | bytes 7864320 | tf_op jit(solution)/shard_map/all_gather | solution.py:24
  9.3 62.5 %copy-start.3 = (s32[1,2,8]{2,1,0:T(2,128)S(1)}, s32[1,2,8]{2,1,0:T(2,128)}, u32[]{:S(2)}) copy-start(s32[1,2,8]{2,1,0:T(2,128)} %param.12) | copy-start | bytes 196
  9.3 312.9 %reduce-scatter.2.cloned.1.call-start = ((), (), s32[]{:S(2)}) async-start(), calls=%async_computation.5 | async-start | bytes 4718592 | tf_op jit(solution)/shard_map/reduce_scatter | solution.py:68
Sparse Core Ops, SparseCore 0:
  9.5 52.1 all-gather.6
  63.3 44.9 all-gather.8
  109.8 46.3 all-gather.10
  157.7 46.3 all-gather.12
  234.3 87.8 reduce-scatter.1
where the time goes:
time: 331 us
  waiting for transfers between devices  207 us (63%)
  blocking collectives  58.7 us (18%)
  matrix products  19.8 us (6%)
  other arithmetic  19.1 us (6%)
  between operations  13.3 us (4%)
  local copies, waits for them, and re-layouts  12.2 us (4%)
    reduce_scatter x1, waiting for transfers between devices, body(): lax.psum_scatter(summed_all, 'expert', scatter_dimension=0, tiled=True)  88.1 us
    all_gather x1, waiting for transfers between devices, expert_ffn(): lax.all_gather(w_down, 'dp', axis=2, tiled=True)  47.8 us
    all_gather x1, waiting for transfers between devices, expert_ffn(): lax.all_gather(w_up, 'dp', axis=1, tiled=True)  41.2 us
    all_gather x1, blocking collectives, body(): lax.all_gather(expert_ids, 'expert', axis=0, tiled=True)  32.5 us
    all_gather x1, waiting for transfers between devices, expert_ffn(): lax.all_gather(w_gate, 'dp', axis=1, tiled=True)  27.6 us
    all_gather x1, blocking collectives, body(): lax.all_gather(gates, 'expert', axis=0, tiled=True)  26.2 us
    scatter-add x1, other arithmetic, body(): jnp.zeros((group_size, width), jnp.float32).at[slot_list.reshape(-1)]  17 us
    dot_general x1, matrix products, expert_ffn(): jnp.einsum('ecf,efd->ecd', hidden, lax.all_gather(w_down, 'dp', axis=2, t...  13.1 us
  transfers between devices with their start and end apart: 5, of which 4 were waited for; matrix products, arithmetic and copies ran while one was open for 6% of the time, Pallas kernels for 0%

commit v1 on v0

--- a/solution.py
+++ b/solution.py
@@ -1,7 +1,270 @@
+import functools
+
 import jax
 import jax.numpy as jnp
 from jax import lax
+from jax.experimental import pallas as pl
+from jax.experimental.pallas import tpu as pltpu
 from jax.sharding import PartitionSpec as P
+
+LANES = 128
+TILE = 256
+
+
+def moe_kernel(
+    peers, ext, wg, wu, wd, out,
+    tok, full_g, full_u, full_d, acc_g, acc_u, hid, part, landed, scale,
+    own_sem, peer_send, peer_recv, sib_send, sib_recv, fwd_send, fwd_recv,
+    tok_send, tok_recv, out_send, out_recv,
+):
+    dp = lax.axis_index("dp")
+    me = lax.axis_index("expert")
+    across = lax.rem(dp + 2, 4)
+    sib = dp + 1 - 2 * lax.rem(dp, 2)
+    diag = lax.rem(sib + 2, 4)
+    rows = ext.shape[0]
+    depth = wg.shape[1]
+    ff = wg.shape[2]
+    mine = pl.ds(pl.multiple_of(me * rows, rows), rows)
+
+    def target(step):
+        return lax.rem(me + step, peers)
+
+    def dev(d, e):
+        return {"dp": d, "expert": e}
+
+    barrier = pltpu.get_barrier_semaphore()
+    pl.semaphore_signal(barrier, inc=1, device_id=dev(across, me), device_id_type=pl.DeviceIdType.MESH)
+    pl.semaphore_signal(barrier, inc=1, device_id=dev(sib, me), device_id_type=pl.DeviceIdType.MESH)
+    for step in range(1, peers):
+        pl.semaphore_signal(barrier, inc=1, device_id=dev(dp, target(step)), device_id_type=pl.DeviceIdType.MESH)
+    pl.semaphore_wait(barrier, peers + 1)
+
+    def part_src(k):
+        if k < 4:
+            return (wg, wu)[k % 2].at[k // 2]
+        return wd.at[:, :, pl.ds((k - 4) * TILE, TILE)]
+
+    def part_dst(k, q):
+        if k < 4:
+            return (full_g, full_u)[k % 2].at[q, k // 2]
+        return full_d.at[q, k - 4]
+
+    n_parts = 6
+
+    def remote(src, dst, s, r, device):
+        return pltpu.make_async_remote_copy(
+            src_ref=src, dst_ref=dst, send_sem=s, recv_sem=r,
+            device_id=device, device_id_type=pl.DeviceIdType.MESH,
+        )
+
+    to_peer = [
+        remote(part_src(k), part_dst(k, dp), peer_send.at[k], peer_recv.at[k], dev(across, me))
+        for k in range(n_parts)
+    ]
+    to_sib = [
+        remote(part_src(k), part_dst(k, dp), sib_send.at[k], sib_recv.at[k], dev(sib, me))
+        for k in range(n_parts)
+    ]
+    forward = [
+        remote(part_dst(k, across), part_dst(k, across), fwd_send.at[k], fwd_recv.at[k], dev(sib, me))
+        for k in range(n_parts)
+    ]
+    local = [
+        pltpu.make_async_copy(part_src(k), part_dst(k, dp), own_sem.at[k]) for k in range(n_parts)
+    ]
+    token_copies = [
+        remote(ext, tok.at[mine], tok_send.at[s - 1], tok_recv.at[s - 1], dev(dp, target(s)))
+        for s in range(1, peers)
+    ]
+
+    to_peer[0].start()
+    to_peer[1].start()
+    for c in token_copies:
+        c.start()
+    for c in local:
+        c.start()
+    for c in to_sib:
+        c.start()
+    tok[mine, :] = ext[...]
+
+    def pass_on(k):
+        to_peer[k].wait_recv()
+        forward[k].start()
+        if k + 2 < n_parts:
+            to_peer[k + 2].start()
+
+    def project(k, q, first):
+        weight, total = ((full_g, acc_g), (full_u, acc_u))[k % 2]
+        j = k // 2
+
+        def tile(t, carry):
+            cols = pl.ds(pl.multiple_of(t * TILE, TILE), TILE)
+            new = jnp.dot(
+                tok[:, pl.ds(pl.multiple_of(q * depth, depth), depth)],
+                weight[q, j, :, cols],
+                preferred_element_type=jnp.float32,
+            )
+            if first:
+                total[j, :, cols] = new
+            else:
+                total[j, :, cols] += new
+            return carry
+
+        lax.fori_loop(0, ff // TILE, tile, 0)
+
+    def activate(j):
+        def tile(t, carry):
+            cols = pl.ds(pl.multiple_of(t * TILE, TILE), TILE)
+            v = acc_g[j, :, cols]
+            hid[j, :, cols] = (v / (1.0 + jnp.exp(-v)) * acc_u[j, :, cols]).astype(jnp.bfloat16)
+            return carry
+
+        lax.fori_loop(0, ff // TILE, tile, 0)
+
+    pass_on(0)
+    for c in token_copies:
+        c.wait_recv()
+    width = 4 * depth
+    table = tok[:, width:].astype(jnp.float32)
+    lane = lax.broadcasted_iota(jnp.int32, table.shape, 1)
+    for j in range(2):
+        one = jnp.sum(jnp.where(lane == 2 * me + j, table, 0.0), axis=1, keepdims=True)
+        scale[j] = jnp.broadcast_to(one, table.shape)
+    for k in range(4):
+        local[k].wait()
+        project(k, dp, True)
+    pass_on(1)
+    for k in range(4):
+        to_sib[k].wait_recv()
+        project(k, sib, False)
+    project(0, across, False)
+    project(1, across, False)
+    for k in (0, 1):
+        forward[k].wait_recv()
+        project(k, diag, False)
+    activate(0)
+    pass_on(2)
+    project(2, across, False)
+    forward[2].wait_recv()
+    project(2, diag, False)
+    pass_on(3)
+    project(3, across, False)
+    forward[3].wait_recv()
+    project(3, diag, False)
+    activate(1)
+
+    sends = []
+
+    def down(h, q, slot):
+        start = pl.multiple_of(q * depth + h * TILE, TILE)
+        cols = pl.ds(start, TILE)
+        total = None
+        for j in range(2):
+            new = jnp.dot(hid[j], full_d[q, h, j], preferred_element_type=jnp.float32)
+            new = new * jnp.concatenate([scale[j]] * (TILE // LANES), axis=1)
+            total = new if total is None else total + new
+        part[:, cols] = total.astype(jnp.bfloat16)
+        for s in range(1, peers):
+            to = target(s)
+            copy = remote(
+                part.at[pl.ds(pl.multiple_of(to * rows, rows), rows), cols],
+                landed.at[s - 1, :, cols],
+                out_send.at[slot, s - 1],
+                out_recv.at[slot, s - 1],
+                dev(dp, to),
+            )
+            copy.start()
+            sends.append(copy)
+
+    def finish(h, q, slot):
+        cols = pl.ds(pl.multiple_of(q * depth + h * TILE, TILE), TILE)
+        for copy in sends[slot * (peers - 1):(slot + 1) * (peers - 1)]:
+            copy.wait_recv()
+        total = part[mine, cols].astype(jnp.float32)
+        for s in range(peers - 1):
+            total += landed[s, :, cols].astype(jnp.float32)
+        out[:, cols] = total.astype(jnp.bfloat16)
+
+    order = []
+
+    def step(h, q):
+        down(h, q, len(order))
+        order.append((h, q))
+
+    local[4].wait()
+    step(0, dp)
+    local[5].wait()
+    step(1, dp)
+    to_sib[4].wait_recv()
+    step(0, sib)
+    to_sib[5].wait_recv()
+    step(1, sib)
+    pass_on(4)
+    step(0, across)
+    forward[4].wait_recv()
+    step(0, diag)
+    pass_on(5)
+    step(1, across)
+    forward[5].wait_recv()
+    step(1, diag)
+    for slot, (h, q) in enumerate(order):
+        finish(h, q, slot)
+
+    for c in to_peer + to_sib + forward + token_copies + sends:
+        c.wait_send()
+
+
+def fits(n_dp, peers, tok_dev, width, per_device, ff):
+    group = tok_dev * peers
+    size = 3 * per_device * width * ff * 2 + group * (width + LANES) * 2
+    size += per_device * group * ff * 10 + 2 * group * width * 2 + per_device * group * LANES * 4
+    return (
+        n_dp == 4 and per_device == 2 and per_device * peers <= LANES and ff % TILE == 0
+        and width == 4 * 2 * TILE and tok_dev % 16 == 0 and size <= 44 * 2**20
+    )
+
+
+def fused(tokens, expert_ids, gates, cap_src, w_gate, w_up, w_down):
+    peers = lax.axis_size("expert")
+    rows, width = tokens.shape
+    per_device, depth, ff = w_gate.shape
+    group = rows * peers
+    numbers = jnp.arange(LANES, dtype=jnp.int32)
+    names = expert_ids[:, :, None] == numbers
+    value = jnp.sum(jnp.where(names, gates.astype(jnp.float32)[:, :, None], 0.0), axis=1)
+    named = jnp.any(names, axis=1).astype(jnp.bfloat16)
+    place = jnp.arange(rows, dtype=jnp.int32)
+    before = (place[:, None] >= place[None, :]).astype(jnp.bfloat16)
+    rank = jnp.dot(before, named, preferred_element_type=jnp.float32)
+    table = jnp.where(rank <= cap_src, value, 0.0).astype(jnp.bfloat16)
+    ext = jnp.concatenate([tokens, table], axis=1)
+    dma = pltpu.SemaphoreType.DMA
+    n_down = width // TILE
+    return pl.pallas_call(
+        functools.partial(moe_kernel, peers),
+        out_shape=jax.ShapeDtypeStruct((rows, width), jnp.bfloat16),
+        in_specs=[pl.BlockSpec(memory_space=pltpu.VMEM)] + [pl.BlockSpec(memory_space=pl.ANY)] * 3,
+        out_specs=pl.BlockSpec(memory_space=pltpu.VMEM),
+        scratch_shapes=[
+            pltpu.VMEM((group, width + LANES), jnp.bfloat16),
+            pltpu.VMEM((4, per_device, depth, ff), jnp.bfloat16),
+            pltpu.VMEM((4, per_device, depth, ff), jnp.bfloat16),
+            pltpu.VMEM((4, depth // TILE, per_device, ff, TILE), jnp.bfloat16),
+            pltpu.VMEM((per_device, group, ff), jnp.float32),
+            pltpu.VMEM((per_device, group, ff), jnp.float32),
+            pltpu.VMEM((per_device, group, ff), jnp.bfloat16),
+            pltpu.VMEM((group, width), jnp.bfloat16),
+            pltpu.VMEM((peers - 1, rows, width), jnp.bfloat16),
+            pltpu.VMEM((per_device, group, LANES), jnp.float32),
+            dma((6,)), dma((6,)), dma((6,)), dma((6,)), dma((6,)), dma((6,)), dma((6,)),
+            dma((peers - 1,)), dma((peers - 1,)),
+            dma((n_down, peers - 1)), dma((n_down, peers - 1)),
+        ],
+        compiler_params=pltpu.CompilerParams(
+            collective_id=0, has_side_effects=True, vmem_limit_bytes=52 * 2**20
+        ),
+    )(ext, w_gate, w_up, w_down)
 
 
 def expert_ffn(token_rows, w_gate, w_up, w_down):
@@ -38,6 +301,8 @@
     cap_e = slot_list.shape[1]
     cap_src = cap_e // peers
     group_size = tok_dev * peers
+    if fits(lax.axis_size("dp"), peers, tok_dev, width, per_device, w_gate.shape[2]):
+        return fused(tokens, expert_ids, gates, cap_src, w_gate, w_up, w_down)
     mine = my_rank * per_device + jnp.arange(per_device, dtype=jnp.int32)
     usable = (jnp.arange(cap_e, dtype=jnp.int32) % cap_src)[None, :] < jnp.repeat(
         counts, cap_src, axis=1

time: 331 us -> 131 us (0.40)
  waiting for transfers between devices: 207 us -> 0 us
  Pallas kernels: 0 us -> 126 us
  blocking collectives: 58.7 us -> 0 us
  matrix products: 19.8 us -> 0.13 us
  other arithmetic: 19.1 us -> 1.36 us
  between operations: 13.3 us -> 0.02 us
  local copies, waits for them, and re-layouts: 12.2 us -> 2.24 us
    pallas_call x0 -> x1, Pallas kernels: none -> 126 us  [fused(): pl.pallas_call(functools.partial(moe_kernel, peers), out_shape=jax.ShapeD...]
    all_gather x4 -> x0, waiting for transfers between devices: 117 us -> none  [the longest x1 47.8 us: expert_ffn(): lax.all_gather(w_down, 'dp', axis=2, tiled=True)]
    reduce_scatter x1 -> x0, waiting for transfers between devices: 88.1 us -> none  [body(): lax.psum_scatter(summed_all, 'expert', scatter_dimension=0, tiled=True)]
    all_gather x2 -> x0, blocking collectives: 58.7 us -> none  [the longest x1 32.5 us: body(): lax.all_gather(expert_ids, 'expert', axis=0, tiled=True)]
    dot_general x2 -> x1, matrix products: 19.8 us -> 0.13 us  [fused(): rank = jnp.dot(before, named, preferred_element_type=jnp.float32)]
    scatter-add x1 -> x0, other arithmetic: 17 us -> none  [body(): jnp.zeros((group_size, width), jnp.float32).at[slot_list.reshape(-1)]]
    gather x3 -> x0, local copies, waits for them, and re-layouts: 11.8 us -> none  [the longest x1 8.36 us: body(): token_rows = group_rows[slot_list]]
  transfers between devices with their start and end apart: 5 -> 0, of which waited for: 4 -> 0; matrix products, arithmetic and copies ran while one was open for 6% -> 0% of each run, Pallas kernels for 0% -> 0%
where the time goes in v1:
time: 131 us; the launch traced here: 130 us
  Pallas kernels  126 us (96%)
  local copies, waits for them, and re-layouts  2.24 us (2%)
  other arithmetic  1.36 us (1%)
    pallas_call x1, Pallas kernels, fused(): pl.pallas_call(functools.partial(moe_kernel, peers), out_shape=jax.ShapeD...  126 us

profile of v1, /device:TPU:0, one launch (start us, length us, event | category | flops | bytes accessed | tf_op | source)
XLA Modules:
  0.0 129.9 jit_solution(10552772477298866562)
XLA Ops:
  0.0 0.8 copy.9
  0.8 0.2 fusion.2
  0.9 0.8 copy.10
  1.7 0.2 select_reduce_fusion
  1.9 0.1 fusion.1
  2.1 1.0 pad_maximum_fusion.ext
  3.0 126.1 %shard_map.64 = bf16[64,2048]{1,0:T(8,128)(2,1)S(1)} custom-call(bf16[64,2176]{1,0:T(8,128)(2,1)S(1)} %pad_maximum_fusion.ext, bf16[2,512,768]{2,1,0:T(8,128)(2,1)} %wg.1, bf16[2,512,768]{2,1,0:T(8,128)(2,1)} %wu.1, bf16[2,768,512]{2,1,0:T(8,128)(2,1)} %wd.1), custom_call_target="tpu_custom_call" | custom-call | tf_op jit(solution)/shard_map/pallas_call | solution.py:244
  129.2 0.7 copy.12

commit v2 on v1

v2 whole, which is shorter than its diff:
```python
import functools

import jax
import jax.numpy as jnp
from jax import lax
from jax.experimental import pallas as pl
from jax.experimental.pallas import tpu as pltpu
from jax.sharding import PartitionSpec as P

LANES = 128
TILE = 256


def moe_kernel(
    peers, cap_src, tokens, ids, gates, wg, wu, wd, out,
    tok, full_g, full_u, full_d, acc_g, acc_u, hid, part, near, paired, landed, scale,
    own_sem, peer_send, peer_recv, sib_send, sib_recv, fwd_send, fwd_recv,
    tok_send, tok_recv, near_send, near_recv, line_send, line_recv, out_send, out_recv,
):
    dp = lax.axis_index("dp")
    me = lax.axis_index("expert")
    across = lax.rem(dp + 2, 4)
    sib = dp + 1 - 2 * lax.rem(dp, 2)
    diag = lax.rem(sib + 2, 4)
    rows, width = tokens.shape
    depth = wg.shape[1]
    ff = wg.shape[2]
    line = peers // 2
    side = lax.rem(me, 2)
    place = lax.div(me, 2)
    mine = pl.ds(pl.multiple_of(me * rows, rows), rows)
    home = pl.ds(pl.multiple_of(place * rows, rows), rows)

    def dev(d, e):
        return {"dp": d, "expert": e}

    def remote(src, dst, s, r, device):
        return pltpu.make_async_remote_copy(
            src_ref=src, dst_ref=dst, send_sem=s, recv_sem=r,
            device_id=device, device_id_type=pl.DeviceIdType.MESH,
        )

    def target(step):
        return lax.rem(me + step, peers)

    barrier = pltpu.get_barrier_semaphore()
    greeted = [dev(across, me), dev(sib, me)] + [dev(dp, target(s)) for s in range(1, peers)]
    for device in greeted:
        pl.semaphore_signal(barrier, inc=1, device_id=device, device_id_type=pl.DeviceIdType.MESH)
    pl.semaphore_wait(barrier, peers + 1)

    n_down = depth // LANES
    n_parts = 4 + n_down

    def part_src(k):
        if k < 4:
            return (wg, wu)[k % 2].at[k // 2]
        return wd.at[:, :, pl.ds((k - 4) * LANES, LANES)]

    def part_dst(k, q):
        if k < 4:
            return (full_g, full_u)[k % 2].at[q, k // 2]
        return full_d.at[q, :, :, pl.ds((k - 4) * LANES, LANES)]

    to_peer = [
        remote(part_src(k), part_dst(k, dp), peer_send.at[k], peer_recv.at[k], dev(across, me))
        for k in range(n_parts)
    ]
    forward = [
        remote(part_dst(k, across), part_dst(k, across), fwd_send.at[k], fwd_recv.at[k], dev(sib, me))
        for k in range(n_parts)
    ]
    whole = ((wg, full_g), (wu, full_u), (wd, full_d))
    to_sib = [
        remote(a, b.at[dp], sib_send.at[i], sib_recv.at[i], dev(sib, me))
        for i, (a, b) in enumerate(whole)
    ]
    local = [pltpu.make_async_copy(a, b.at[dp], own_sem.at[i]) for i, (a, b) in enumerate(whole)]
    token_copies = [
        remote(tok.at[mine], tok.at[mine], tok_send.at[s - 1], tok_recv.at[s - 1], dev(dp, target(s)))
        for s in range(1, peers)
    ]

    AHEAD = 3
    for k in range(AHEAD):
        to_peer[k].start()
    tok[mine, :width] = tokens[...]
    gate_vals = gates[...].astype(jnp.float32)
    chosen = ids[...]
    number = lax.broadcasted_iota(jnp.int32, (LANES, rows), 0)
    value = jnp.zeros((LANES, rows), jnp.float32)
    named = jnp.zeros((LANES, rows), jnp.float32)
    for k in range(chosen.shape[0]):
        hit = number == chosen[k:k + 1, :]
        value += jnp.where(hit, gate_vals[k:k + 1, :], 0.0)
        named += jnp.where(hit, 1.0, 0.0)
    first = lax.broadcasted_iota(jnp.int32, (rows, rows), 0)
    second = lax.broadcasted_iota(jnp.int32, (rows, rows), 1)
    upto = jnp.where(first <= second, 1.0, 0.0).astype(jnp.bfloat16)
    unit = jnp.where(first == second, 1.0, 0.0).astype(jnp.bfloat16)
    rank = jnp.dot(named.astype(jnp.bfloat16), upto, preferred_element_type=jnp.float32)
    kept = jnp.where(rank <= cap_src, value, 0.0).astype(jnp.bfloat16)
    tok[mine, width:] = lax.dot_general(
        unit, kept, (((1,), (1,)), ((), ())), preferred_element_type=jnp.float32
    ).astype(jnp.bfloat16)
    for c in token_copies:
        c.start()
    for c in local:
        c.start()
    for c in to_sib:
        c.start()

    def pass_on(k):
        to_peer[k].wait_recv()
        forward[k].start()
        if k + AHEAD < n_parts:
            to_peer[k + AHEAD].start()

    def project(k, q, first):
        weight, total = ((full_g, acc_g), (full_u, acc_u))[k % 2]
        j = k // 2

        def tile(t, carry):
            cols = pl.ds(pl.multiple_of(t * TILE, TILE), TILE)
            new = jnp.dot(
                tok[:, pl.ds(pl.multiple_of(q * depth, depth), depth)],
                weight[q, j, :, cols],
                preferred_element_type=jnp.float32,
            )
            if first:
                total[j, :, cols] = new
            else:
                total[j, :, cols] += new
            return carry

        lax.fori_loop(0, ff // TILE, tile, 0)

    def activate(j):
        def tile(t, carry):
            cols = pl.ds(pl.multiple_of(t * TILE, TILE), TILE)
            v = acc_g[j, :, cols]
            hid[j, :, cols] = (v / (1.0 + jnp.exp(-v)) * acc_u[j, :, cols]).astype(jnp.bfloat16)
            return carry

        lax.fori_loop(0, ff // TILE, tile, 0)

    pass_on(0)
    for c in token_copies:
        c.wait_recv()
    pass_on(1)
    table = tok[:, width:].astype(jnp.float32)
    lane = lax.broadcasted_iota(jnp.int32, table.shape, 1)
    for j in range(2):
        one = jnp.sum(jnp.where(lane == 2 * me + j, table, 0.0), axis=1, keepdims=True)
        scale[j] = jnp.broadcast_to(one, table.shape)
    for m in range(2):
        local[m].wait()
        project(m, dp, True)
        project(m + 2, dp, True)
    for m in range(2):
        to_sib[m].wait_recv()
        project(m, sib, False)
        project(m + 2, sib, False)
    for k in (0, 1):
        project(k, across, False)
    for k in (0, 1):
        forward[k].wait_recv()
        project(k, diag, False)
    pass_on(2)
    activate(0)
    project(2, across, False)
    forward[2].wait_recv()
    project(2, diag, False)
    pass_on(3)
    project(3, across, False)
    forward[3].wait_recv()
    project(3, diag, False)
    activate(1)

    def down(q, at, size):
        cols = pl.ds(pl.multiple_of(q * depth + at, size), size)
        total = None
        for j in range(2):
            new = jnp.dot(
                hid[j], full_d[q, j, :, pl.ds(at, size)], preferred_element_type=jnp.float32
            )
            new = new * jnp.concatenate([scale[j]] * (size // LANES), axis=1)
            total = new if total is None else total + new
        total = total.astype(jnp.bfloat16)
        for e in range(peers):
            part[e % 2, (e // 2) * rows:(e // 2 + 1) * rows, cols] = total[e * rows:(e + 1) * rows]
        return cols

    pairs, lines, direct = [], [], []

    def near_step(q, at):
        slot = len(pairs)
        cols = down(q, at, TILE)
        copy = remote(
            part.at[1 - side, :, cols], near.at[:, cols],
            near_send.at[slot], near_recv.at[slot], dev(dp, me + 1 - 2 * side),
        )
        copy.start()
        pairs.append((copy, cols))

    def line_step(slot):
        copy, cols = pairs[slot]
        copy.wait_recv()
        both = part[side, :, cols].astype(jnp.float32) + near[:, cols].astype(jnp.float32)
        paired[:, cols] = both.astype(jnp.bfloat16)
        sent = []
        for s in range(1, line):
            to = lax.rem(place + s, line)
            send = remote(
                paired.at[pl.ds(pl.multiple_of(to * rows, rows), rows), cols],
                landed.at[s - 1, :, cols],
                line_send.at[slot, s - 1], line_recv.at[slot, s - 1], dev(dp, 2 * to + side),
            )
            send.start()
            sent.append(send)
        lines.append(sent)

    def direct_step(q, at):
        slot = len(direct)
        cols = down(q, at, LANES)
        sent = []
        for s in range(1, peers):
            to = target(s)
            send = remote(
                part.at[lax.rem(to, 2), pl.ds(pl.multiple_of(lax.div(to, 2) * rows, rows), rows), cols],
                landed.at[s - 1, :, cols],
                out_send.at[slot, s - 1], out_recv.at[slot, s - 1], dev(dp, to),
            )
            send.start()
            sent.append(send)
        direct.append((sent, cols))

    def finish(sent, cols, own):
        for send in sent:
            send.wait_recv()
        total = own.astype(jnp.float32)
        for s in range(len(sent)):
            total += landed[s, :, cols].astype(jnp.float32)
        out[:, cols] = total.astype(jnp.bfloat16)

    def finish_line(slot):
        cols = pairs[slot][1]
        finish(lines[slot], cols, paired[home, cols])

    def finish_direct(slot):
        sent, cols = direct[slot]
        finish(sent, cols, part[side, home, cols])

    local[2].wait()
    near_step(dp, 0)
    near_step(dp, TILE)
    to_sib[2].wait_recv()
    near_step(sib, 0)
    near_step(sib, TILE)
    line_step(0)
    line_step(1)
    for c in range(n_down):
        pass_on(4 + c)
        if c == 0:
            line_step(2)
            line_step(3)
        direct_step(across, c * LANES)
        forward[4 + c].wait_recv()
        direct_step(diag, c * LANES)
        if c == 1:
            for slot in range(4):
                finish_line(slot)
        if c == 2:
            finish_direct(0)
            finish_direct(1)
    for slot in range(2, 2 * n_down):
        finish_direct(slot)

    for c in to_peer + to_sib + forward + token_copies:
        c.wait_send()
    for copy, unused in pairs:
        copy.wait_send()
    for sent in lines + [d[0] for d in direct]:
        for send in sent:
            send.wait_send()


def fits(n_dp, peers, tok_dev, width, per_device, ff):
    group = tok_dev * peers
    size = 3 * per_device * width * ff * 2 + group * (width + LANES) * 2
    size += per_device * group * ff * 10 + 3 * group * width * 2 + per_device * group * LANES * 4
    return (
        n_dp == 4 and per_device == 2 and per_device * peers <= LANES and ff % TILE == 0
        and width == 4 * 2 * TILE and tok_dev % 16 == 0 and tok_dev <= LANES
        and peers % 2 == 0 and peers >= 4 and size <= 46 * 2**20
    )


def fused(tokens, expert_ids, gates, cap_src, w_gate, w_up, w_down):
    peers = lax.axis_size("expert")
    rows, width = tokens.shape
    per_device, depth, ff = w_gate.shape
    group = rows * peers
    dma = pltpu.SemaphoreType.DMA
    n_parts = 4 + depth // LANES
    vmem = pl.BlockSpec(memory_space=pltpu.VMEM)
    return pl.pallas_call(
        functools.partial(moe_kernel, peers, cap_src),
        out_shape=jax.ShapeDtypeStruct((rows, width), jnp.bfloat16),
        in_specs=[vmem] * 3 + [pl.BlockSpec(memory_space=pl.ANY)] * 3,
        out_specs=vmem,
        scratch_shapes=[
            pltpu.VMEM((group, width + LANES), jnp.bfloat16),
            pltpu.VMEM((4, per_device, depth, ff), jnp.bfloat16),
            pltpu.VMEM((4, per_device, depth, ff), jnp.bfloat16),
            pltpu.VMEM((4, per_device, ff, depth), jnp.bfloat16),
            pltpu.VMEM((per_device, group, ff), jnp.float32),
            pltpu.VMEM((per_device, group, ff), jnp.float32),
            pltpu.VMEM((per_device, group, ff), jnp.bfloat16),
            pltpu.VMEM((2, group // 2, width), jnp.bfloat16),
            pltpu.VMEM((group // 2, width), jnp.bfloat16),
            pltpu.VMEM((group // 2, width), jnp.bfloat16),
            pltpu.VMEM((peers - 1, rows, width), jnp.bfloat16),
            pltpu.VMEM((per_device, group, LANES), jnp.float32),
            dma((3,)), dma((n_parts,)), dma((n_parts,)), dma((3,)), dma((3,)),
            dma((n_parts,)), dma((n_parts,)),
            dma((peers - 1,)), dma((peers - 1,)),
            dma((4,)), dma((4,)),
            dma((4, peers // 2 - 1)), dma((4, peers // 2 - 1)),
            dma((2 * (depth // LANES), peers - 1)), dma((2 * (depth // LANES), peers - 1)),
        ],
        compiler_params=pltpu.CompilerParams(
            collective_id=0, has_side_effects=True, vmem_limit_bytes=54 * 2**20
        ),
    )(tokens, expert_ids.T, gates.T, w_gate, w_up, w_down)


def expert_ffn(token_rows, w_gate, w_up, w_down):
    gate_new = jnp.einsum(
        "ecd,edf->ecf",
        token_rows,
        lax.all_gather(w_gate, "dp", axis=1, tiled=True),
        preferred_element_type=jnp.float32,
    )
    up_new = jnp.einsum(
        "ecd,edf->ecf",
        token_rows,
        lax.all_gather(w_up, "dp", axis=1, tiled=True),
        preferred_element_type=jnp.float32,
    )
    hidden = (jax.nn.silu(gate_new) * up_new).astype(jnp.bfloat16)
    return jnp.einsum(
        "ecf,efd->ecd",
        hidden,
        lax.all_gather(w_down, "dp", axis=2, tiled=True),
        preferred_element_type=jnp.float32,
    )


def body(tokens, expert_ids, gates, kept_token, kept_count, w_gate, w_up, w_down):
    my_rank = lax.axis_index("expert")
    peers = lax.axis_size("expert")
    per_device = w_gate.shape[0]
    tok_dev = tokens.shape[0]
    width = tokens.shape[1]
    top_count = expert_ids.shape[1]
    slot_list = kept_token[0]
    counts = kept_count[0]
    cap_e = slot_list.shape[1]
    cap_src = cap_e // peers
    group_size = tok_dev * peers
    if fits(lax.axis_size("dp"), peers, tok_dev, width, per_device, w_gate.shape[2]):
        return fused(tokens, expert_ids, gates, cap_src, w_gate, w_up, w_down)
    mine = my_rank * per_device + jnp.arange(per_device, dtype=jnp.int32)
    usable = (jnp.arange(cap_e, dtype=jnp.int32) % cap_src)[None, :] < jnp.repeat(
        counts, cap_src, axis=1
    )
    start_bufs = (
        jnp.zeros((group_size, width), jnp.bfloat16),
        jnp.zeros((group_size, top_count), jnp.int32),
        jnp.zeros((group_size, top_count), jnp.bfloat16),
    )
    pieces = (
        lax.all_gather(tokens, "expert", axis=0, tiled=True),
        lax.all_gather(expert_ids, "expert", axis=0, tiled=True),
        lax.all_gather(gates, "expert", axis=0, tiled=True),
    )
    first_row = jnp.int32(0)
    group_rows, group_ids, group_gates = tuple(
        (lax.dynamic_update_slice_in_dim(start_bufs[i], pieces[i], first_row, 0) for i in range(3))
    )
    token_rows = group_rows[slot_list]
    names_it = group_ids[slot_list] == mine[:, None, None]
    slot_weight = jnp.sum(
        jnp.where(names_it, group_gates[slot_list].astype(jnp.float32), 0.0), axis=2
    )
    slot_weight = jnp.where(usable, slot_weight, 0.0)
    outputs = expert_ffn(token_rows, w_gate, w_up, w_down)
    flat_out = (outputs * slot_weight[:, :, None]).reshape(-1, width)
    summed_all = jnp.zeros((group_size, width), jnp.float32).at[slot_list.reshape(-1)].add(flat_out)
    return lax.psum_scatter(summed_all, "expert", scatter_dimension=0, tiled=True).astype(
        jnp.bfloat16
    )


def solution(mesh):
    return jax.shard_map(
        body,
        mesh=mesh,
        in_specs=(
            P(("dp", "expert"), None),
            P(("dp", "expert"), None),
            P(("dp", "expert"), None),
            P("dp", "expert", None),
            P("dp", "expert", None),
            P("expert", "dp", None),
            P("expert", "dp", None),
            P("expert", None, "dp"),
        ),
        out_specs=P(("dp", "expert"), None),
        check_vma=False,
    )
```

time: 131 us -> 125 us (0.954)
  Pallas kernels: 126 us -> 123 us
  other arithmetic: 1.36 us -> 0 us
    pallas_call x1, Pallas kernels: 126 us -> 123 us  [fused(): pl.pallas_call(functools.partial(moe_kernel, peers, cap_src), out_shape=j...]
where the time goes in v2:
time: 125 us
  Pallas kernels  123 us (98%)
  local copies, waits for them, and re-layouts  1.67 us (1%)
    pallas_call x1, Pallas kernels, fused(): pl.pallas_call(functools.partial(moe_kernel, peers, cap_src), out_shape=j...  123 us

profile of v2, /device:TPU:0, one launch (start us, length us, event | category | flops | bytes accessed | tf_op | source)
XLA Modules:
  0.0 124.8 jit_solution(14639134886348554382)
XLA Ops:
  0.0 123.1 %shard_map.64 = bf16[64,2048]{1,0:T(8,128)(2,1)} custom-call(bf16[64,2048]{1,0:T(8,128)(2,1)} %tokens.1, s32[8,64]{1,0:T(8,128)} %bitcast.2, bf16[8,64]{1,0:T(8,128)(2,1)} %bitcast.3, bf16[2,512,768]{2,1,0:T(8,128)(2,1)} %wg.1, bf16[2,512,768]{2,1,0:T(8,128)(2,1)} %wu.1, bf16[2,768,512]{2,1,0:T(8,128)(2,1)} %wd.1), custom_call_target="tpu_custom_call" | custom-call | tf_op jit(solution)/shard_map/pallas_call | solution.py:307
  123.1 1.7 %copy.8 = bf16[64,2048]{1,0:T(8,128)(2,1)} copy(bf16[64,2048]{1,0:T(8,128)(2,1)} %shard_map.64) | data formatting | bytes 524288

commit v3 on v2

--- a/solution.py
+++ b/solution.py
@@ -13,9 +13,10 @@
 
 def moe_kernel(
     peers, cap_src, tokens, ids, gates, wg, wu, wd, out,
-    tok, full_g, full_u, full_d, acc_g, acc_u, hid, part, near, paired, landed, scale,
+    tok, full_g, full_u, full_d, acc_g, acc_u, hid, hid_out, part, near, paired, landed, scale,
     own_sem, peer_send, peer_recv, sib_send, sib_recv, fwd_send, fwd_recv,
-    tok_send, tok_recv, near_send, near_recv, line_send, line_recv, out_send, out_recv,
+    cross_send, cross_recv, tline_send, tline_recv, tpair_send, tpair_recv,
+    near_send, near_recv, line_send, line_recv,
 ):
     dp = lax.axis_index("dp")
     me = lax.axis_index("expert")
@@ -29,6 +30,8 @@
     side = lax.rem(me, 2)
     place = lax.div(me, 2)
     mine = pl.ds(pl.multiple_of(me * rows, rows), rows)
+    level = lax.div(dp, 2)
+    beside = me + 1 - 2 * side
     home = pl.ds(pl.multiple_of(place * rows, rows), rows)
 
     def dev(d, e):
@@ -40,27 +43,28 @@
             device_id=device, device_id_type=pl.DeviceIdType.MESH,
         )
 
-    def target(step):
-        return lax.rem(me + step, peers)
+    def along(step):
+        return 2 * lax.rem(place + step, line) + side
 
     barrier = pltpu.get_barrier_semaphore()
-    greeted = [dev(across, me), dev(sib, me)] + [dev(dp, target(s)) for s in range(1, peers)]
+    greeted = [dev(across, me), dev(sib, me), dev(dp, beside)]
+    greeted += [dev(dp, along(s)) for s in range(1, line)]
     for device in greeted:
         pl.semaphore_signal(barrier, inc=1, device_id=device, device_id_type=pl.DeviceIdType.MESH)
-    pl.semaphore_wait(barrier, peers + 1)
+    pl.semaphore_wait(barrier, len(greeted))
 
     n_down = depth // LANES
-    n_parts = 4 + n_down
+    n_parts = 2 + n_down
 
     def part_src(k):
-        if k < 4:
-            return (wg, wu)[k % 2].at[k // 2]
-        return wd.at[:, :, pl.ds((k - 4) * LANES, LANES)]
+        if k < 2:
+            return (wg, wu)[k].at[1 - level]
+        return wd.at[:, :, pl.ds((k - 2) * LANES, LANES)]
 
     def part_dst(k, q):
-        if k < 4:
-            return (full_g, full_u)[k % 2].at[q, k // 2]
-        return full_d.at[q, :, :, pl.ds((k - 4) * LANES, LANES)]
+        if k < 2:
+            return (full_g, full_u)[k].at[q]
+        return full_d.at[q, :, :, pl.ds((k - 2) * LANES, LANES)]
 
     to_peer = [
         remote(part_src(k), part_dst(k, dp), peer_send.at[k], peer_recv.at[k], dev(across, me))
@@ -70,21 +74,53 @@
         remote(part_dst(k, across), part_dst(k, across), fwd_send.at[k], fwd_recv.at[k], dev(sib, me))
         for k in range(n_parts)
     ]
-    whole = ((wg, full_g), (wu, full_u), (wd, full_d))
+    whole = ((wg.at[level], full_g), (wu.at[level], full_u), (wd, full_d))
     to_sib = [
         remote(a, b.at[dp], sib_send.at[i], sib_recv.at[i], dev(sib, me))
         for i, (a, b) in enumerate(whole)
     ]
     local = [pltpu.make_async_copy(a, b.at[dp], own_sem.at[i]) for i, (a, b) in enumerate(whole)]
-    token_copies = [
-        remote(tok.at[mine], tok.at[mine], tok_send.at[s - 1], tok_recv.at[s - 1], dev(dp, target(s)))
-        for s in range(1, peers)
+    def block(g, e):
+        at = pl.ds(pl.multiple_of(e * rows, rows), rows)
+        return tok.at[0, at] if g == 0 else tok.at[1, at, pl.ds(0, width)]
+
+    token_over = remote(
+        tokens, block(1, me), cross_send.at[0], cross_recv.at[0], dev(across, me)
+    )
+    hidden_over = remote(
+        hid_out, hid.at[level], cross_send.at[1], cross_recv.at[1], dev(across, me)
+    )
+    token_line = [
+        [
+            remote(block(g, me), block(g, me), tline_send.at[g, s - 1], tline_recv.at[g, s - 1],
+                   dev(dp, along(s)))
+            for s in range(1, line)
+        ]
+        for g in range(2)
     ]
-
-    AHEAD = 3
+    token_pair = [
+        [
+            remote(block(g, along(line - s)), block(g, along(line - s)), tpair_send.at[g, s],
+                   tpair_recv.at[g, s], dev(dp, beside))
+            for s in range(line)
+        ]
+        for g in range(2)
+    ]
+
+    def spread(g):
+        for c in token_line[g]:
+            c.start()
+        token_pair[g][0].start()
+
+    def relay(g, s):
+        token_line[g][s - 1].wait_recv()
+        token_pair[g][s].start()
+
+    AHEAD = 2
+    token_over.start()
     for k in range(AHEAD):
         to_peer[k].start()
-    tok[mine, :width] = tokens[...]
+    tok[0, mine, :width] = tokens[...]
     gate_vals = gates[...].astype(jnp.float32)
     chosen = ids[...]
     number = lax.broadcasted_iota(jnp.int32, (LANES, rows), 0)
@@ -100,11 +136,9 @@
     unit = jnp.where(first == second, 1.0, 0.0).astype(jnp.bfloat16)
     rank = jnp.dot(named.astype(jnp.bfloat16), upto, preferred_element_type=jnp.float32)
     kept = jnp.where(rank <= cap_src, value, 0.0).astype(jnp.bfloat16)
-    tok[mine, width:] = lax.dot_general(
+    tok[0, mine, width:] = lax.dot_general(
         unit, kept, (((1,), (1,)), ((), ())), preferred_element_type=jnp.float32
     ).astype(jnp.bfloat16)
-    for c in token_copies:
-        c.start()
     for c in local:
         c.start()
     for c in to_sib:
@@ -116,66 +150,76 @@
         if k + AHEAD < n_parts:
             to_peer[k + AHEAD].start()
 
-    def project(k, q, first):
-        weight, total = ((full_g, acc_g), (full_u, acc_u))[k % 2]
-        j = k // 2
-
+    def project(g, q, first):
+        for weight, total in ((full_g, acc_g), (full_u, acc_u)):
+
+            def tile(t, carry):
+                cols = pl.ds(pl.multiple_of(t * TILE, TILE), TILE)
+                new = jnp.dot(
+                    tok[g, :, pl.ds(pl.multiple_of(q * depth, depth), depth)],
+                    weight[q, :, cols],
+                    preferred_element_type=jnp.float32,
+                )
+                if first:
+                    total[:, cols] = new
+                else:
+                    total[:, cols] += new
+                return carry
+
+            lax.fori_loop(0, ff // TILE, tile, 0)
+
+    def activate(store):
         def tile(t, carry):
             cols = pl.ds(pl.multiple_of(t * TILE, TILE), TILE)
-            new = jnp.dot(
-                tok[:, pl.ds(pl.multiple_of(q * depth, depth), depth)],
-                weight[q, j, :, cols],
-                preferred_element_type=jnp.float32,
-            )
-            if first:
-                total[j, :, cols] = new
-            else:
-                total[j, :, cols] += new
+            v = acc_g[:, cols]
+            store(cols, (v / (1.0 + jnp.exp(-v)) * acc_u[:, cols]).astype(jnp.bfloat16))
             return carry
 
         lax.fori_loop(0, ff // TILE, tile, 0)
 
-    def activate(j):
-        def tile(t, carry):
-            cols = pl.ds(pl.multiple_of(t * TILE, TILE), TILE)
-            v = acc_g[j, :, cols]
-            hid[j, :, cols] = (v / (1.0 + jnp.exp(-v)) * acc_u[j, :, cols]).astype(jnp.bfloat16)
-            return carry
-
-        lax.fori_loop(0, ff // TILE, tile, 0)
-
+    def keep_out(cols, rows_out):
+        hid_out[:, cols] = rows_out
+
+    def keep_own(cols, rows_own):
+        hid[level, :, cols] = rows_own
+
+    token_over.wait_recv()
+    spread(1)
+    spread(0)
     pass_on(0)
-    for c in token_copies:
+    for s in range(1, line):
+        relay(1, s)
+    relay(0, 1)
+    pass_on(1)
+    for c in token_pair[1]:
         c.wait_recv()
-    pass_on(1)
-    table = tok[:, width:].astype(jnp.float32)
+    for m in range(2):
+        local[m].wait()
+    project(1, dp, True)
+    for m in range(2):
+        to_sib[m].wait_recv()
+    project(1, sib, False)
+    project(1, across, False)
+    for k in range(2):
+        forward[k].wait_recv()
+    project(1, diag, False)
+    activate(keep_out)
+    hidden_over.start()
+    for s in range(2, line):
+        relay(0, s)
+    pass_on(2)
+    for c in token_pair[0]:
+        c.wait_recv()
+    for i, q in enumerate((dp, sib, across, diag)):
+        project(0, q, i == 0)
+    activate(keep_own)
+    table = tok[0, :, width:].astype(jnp.float32)
     lane = lax.broadcasted_iota(jnp.int32, table.shape, 1)
     for j in range(2):
         one = jnp.sum(jnp.where(lane == 2 * me + j, table, 0.0), axis=1, keepdims=True)
         scale[j] = jnp.broadcast_to(one, table.shape)
-    for m in range(2):
-        local[m].wait()
-        project(m, dp, True)
-        project(m + 2, dp, True)
-    for m in range(2):
-        to_sib[m].wait_recv()
-        project(m, sib, False)
-        project(m + 2, sib, False)
-    for k in (0, 1):
-        project(k, across, False)
-    for k in (0, 1):
-        forward[k].wait_recv()
-        project(k, diag, False)
-    pass_on(2)
-    activate(0)
-    project(2, across, False)
-    forward[2].wait_recv()
-    project(2, diag, False)
     pass_on(3)
-    project(3, across, False)
-    forward[3].wait_recv()
-    project(3, diag, False)
-    activate(1)
+    hidden_over.wait_recv()
 
     def down(q, at, size):
         cols = pl.ds(pl.multiple_of(q * depth + at, size), size)
@@ -191,17 +235,22 @@
             part[e % 2, (e // 2) * rows:(e // 2 + 1) * rows, cols] = total[e * rows:(e + 1) * rows]
         return cols
 
-    pairs, lines, direct = [], [], []
-
-    def near_step(q, at):
+    pairs, lines = [], []
+
+    def near_step(q, at, size, lag):
         slot = len(pairs)
-        cols = down(q, at, TILE)
+        cols = down(q, at, size)
         copy = remote(
             part.at[1 - side, :, cols], near.at[:, cols],
-            near_send.at[slot], near_recv.at[slot], dev(dp, me + 1 - 2 * side),
+            near_send.at[slot], near_recv.at[slot], dev(dp, beside),
         )
         copy.start()
         pairs.append((copy, cols))
+        flush(lag)
+
+    def flush(lag):
+        while len(pairs) - len(lines) > lag:
+            line_step(len(lines))
 
     def line_step(slot):
         copy, cols = pairs[slot]
@@ -220,21 +269,6 @@
             sent.append(send)
         lines.append(sent)
 
-    def direct_step(q, at):
-        slot = len(direct)
-        cols = down(q, at, LANES)
-        sent = []
-        for s in range(1, peers):
-            to = target(s)
-            send = remote(
-                part.at[lax.rem(to, 2), pl.ds(pl.multiple_of(lax.div(to, 2) * rows, rows), rows), cols],
-                landed.at[s - 1, :, cols],
-                out_send.at[slot, s - 1], out_recv.at[slot, s - 1], dev(dp, to),
-            )
-            send.start()
-            sent.append(send)
-        direct.append((sent, cols))
-
     def finish(sent, cols, own):
         for send in sent:
             send.wait_recv()
@@ -247,40 +281,34 @@
         cols = pairs[slot][1]
         finish(lines[slot], cols, paired[home, cols])
 
-    def finish_direct(slot):
-        sent, cols = direct[slot]
-        finish(sent, cols, part[side, home, cols])
-
     local[2].wait()
-    near_step(dp, 0)
-    near_step(dp, TILE)
+    near_step(dp, 0, TILE, 3)
+    near_step(dp, TILE, TILE, 3)
     to_sib[2].wait_recv()
-    near_step(sib, 0)
-    near_step(sib, TILE)
-    line_step(0)
-    line_step(1)
+    near_step(sib, 0, TILE, 3)
+    near_step(sib, TILE, TILE, 3)
     for c in range(n_down):
-        pass_on(4 + c)
-        if c == 0:
-            line_step(2)
-            line_step(3)
-        direct_step(across, c * LANES)
-        forward[4 + c].wait_recv()
-        direct_step(diag, c * LANES)
-        if c == 1:
+        if c == n_down - 1:
+            flush(0)
             for slot in range(4):
                 finish_line(slot)
-        if c == 2:
-            finish_direct(0)
-            finish_direct(1)
-    for slot in range(2, 2 * n_down):
-        finish_direct(slot)
-
-    for c in to_peer + to_sib + forward + token_copies:
+        if c >= 2:
+            pass_on(2 + c)
+        near_step(across, c * LANES, LANES, 3)
+        forward[2 + c].wait_recv()
+        near_step(diag, c * LANES, LANES, 3)
+    flush(0)
+    for slot in range(4, len(pairs)):
+        finish_line(slot)
+
+    for c in to_peer + to_sib + forward + [token_over, hidden_over]:
         c.wait_send()
+    for g in range(2):
+        for c in token_line[g] + token_pair[g]:
+            c.wait_send()
     for copy, unused in pairs:
         copy.wait_send()
-    for sent in lines + [d[0] for d in direct]:
+    for sent in lines:
         for send in sent:
             send.wait_send()
 
@@ -302,7 +330,9 @@
     per_device, depth, ff = w_gate.shape
     group = rows * peers
     dma = pltpu.SemaphoreType.DMA
-    n_parts = 4 + depth // LANES
+    n_parts = 2 + depth // LANES
+    n_slots = 4 + 2 * (depth // LANES)
+    line = peers // 2
     vmem = pl.BlockSpec(memory_space=pltpu.VMEM)
     return pl.pallas_call(
         functools.partial(moe_kernel, peers, cap_src),
@@ -310,24 +340,25 @@
         in_specs=[vmem] * 3 + [pl.BlockSpec(memory_space=pl.ANY)] * 3,
         out_specs=vmem,
         scratch_shapes=[
-            pltpu.VMEM((group, width + LANES), jnp.bfloat16),
-            pltpu.VMEM((4, per_device, depth, ff), jnp.bfloat16),
-            pltpu.VMEM((4, per_device, depth, ff), jnp.bfloat16),
+            pltpu.VMEM((2, group, width + LANES), jnp.bfloat16),
+            pltpu.VMEM((4, depth, ff), jnp.bfloat16),
+            pltpu.VMEM((4, depth, ff), jnp.bfloat16),
             pltpu.VMEM((4, per_device, ff, depth), jnp.bfloat16),
-            pltpu.VMEM((per_device, group, ff), jnp.float32),
-            pltpu.VMEM((per_device, group, ff), jnp.float32),
+            pltpu.VMEM((group, ff), jnp.float32),
+            pltpu.VMEM((group, ff), jnp.float32),
             pltpu.VMEM((per_device, group, ff), jnp.bfloat16),
+            pltpu.VMEM((group, ff), jnp.bfloat16),
             pltpu.VMEM((2, group // 2, width), jnp.bfloat16),
             pltpu.VMEM((group // 2, width), jnp.bfloat16),
             pltpu.VMEM((group // 2, width), jnp.bfloat16),
-            pltpu.VMEM((peers - 1, rows, width), jnp.bfloat16),
+            pltpu.VMEM((line - 1, rows, width), jnp.bfloat16),
             pltpu.VMEM((per_device, group, LANES), jnp.float32),
             dma((3,)), dma((n_parts,)), dma((n_parts,)), dma((3,)), dma((3,)),
             dma((n_parts,)), dma((n_parts,)),
-            dma((peers - 1,)), dma((peers - 1,)),
-            dma((4,)), dma((4,)),
-            dma((4, peers // 2 - 1)), dma((4, peers // 2 - 1)),
-            dma((2 * (depth // LANES), peers - 1)), dma((2 * (depth // LANES), peers - 1)),
+            dma((2,)), dma((2,)),
+            dma((2, line - 1)), dma((2, line - 1)), dma((2, line)), dma((2, line)),
+            dma((n_slots,)), dma((n_slots,)),
+            dma((n_slots, line - 1)), dma((n_slots, line - 1)),
         ],
         compiler_params=pltpu.CompilerParams(
             collective_id=0, has_side_effects=True, vmem_limit_bytes=54 * 2**20

time: 125 us -> 116 us (0.928)
  Pallas kernels: 123 us -> 114 us
    pallas_call x1, Pallas kernels: 123 us -> 114 us  [fused(): pl.pallas_call(functools.partial(moe_kernel, peers, cap_src), out_shape=j...]
where the time goes in v3:
time: 116 us; the launch traced here: 115 us
  Pallas kernels  114 us (98%)
  local copies, waits for them, and re-layouts  1.67 us (1%)
    pallas_call x1, Pallas kernels, fused(): pl.pallas_call(functools.partial(moe_kernel, peers, cap_src), out_shape=j...  114 us

profile of v3, /device:TPU:0, one launch (start us, length us, event | category | flops | bytes accessed | tf_op | source)
XLA Modules:
  0.0 115.4 jit_solution(10478249427298552573)
XLA Ops:
  0.0 113.7 %shard_map.64 = bf16[64,2048]{1,0:T(8,128)(2,1)} custom-call(bf16[64,2048]{1,0:T(8,128)(2,1)} %tokens.1, s32[8,64]{1,0:T(8,128)} %bitcast.2, bf16[8,64]{1,0:T(8,128)(2,1)} %bitcast.3, bf16[2,512,768]{2,1,0:T(8,128)(2,1)} %wg.1, bf16[2,512,768]{2,1,0:T(8,128)(2,1)} %wu.1, bf16[2,768,512]{2,1,0:T(8,128)(2,1)} %wd.1), custom_call_target="tpu_custom_call" | custom-call | tf_op jit(solution)/shard_map/pallas_call | solution.py:337
  113.8 1.7 %copy.8 = bf16[64,2048]{1,0:T(8,128)(2,1)} copy(bf16[64,2048]{1,0:T(8,128)(2,1)} %shard_map.64) | data formatting | bytes 524288

commit v4 on v3

--- a/solution.py
+++ b/solution.py
@@ -288,17 +288,13 @@
     near_step(sib, 0, TILE, 3)
     near_step(sib, TILE, TILE, 3)
     for c in range(n_down):
-        if c == n_down - 1:
-            flush(0)
-            for slot in range(4):
-                finish_line(slot)
         if c >= 2:
             pass_on(2 + c)
         near_step(across, c * LANES, LANES, 3)
         forward[2 + c].wait_recv()
         near_step(diag, c * LANES, LANES, 3)
     flush(0)
-    for slot in range(4, len(pairs)):
+    for slot in range(len(pairs)):
         finish_line(slot)
 
     for c in to_peer + to_sib + forward + [token_over, hidden_over]:

time: 116 us -> 114 us (0.983)
    pallas_call x1, Pallas kernels: 114 us -> 113 us  [fused(): pl.pallas_call(functools.partial(moe_kernel, peers, cap_src), out_shape=j...]
where the time goes in v4:
time: 114 us
  Pallas kernels  113 us (99%)
  local copies, waits for them, and re-layouts  1.67 us (1%)
    pallas_call x1, Pallas kernels, fused(): pl.pallas_call(functools.partial(moe_kernel, peers, cap_src), out_shape=j...  113 us

profile of v4, /device:TPU:0, one launch (start us, length us, event | category | flops | bytes accessed | tf_op | source)
XLA Modules:
  0.0 114.2 jit_solution(8115979916809792125)
XLA Ops:
  0.0 112.5 %shard_map.64 = bf16[64,2048]{1,0:T(8,128)(2,1)} custom-call(bf16[64,2048]{1,0:T(8,128)(2,1)} %tokens.1, s32[8,64]{1,0:T(8,128)} %bitcast.2, bf16[8,64]{1,0:T(8,128)(2,1)} %bitcast.3, bf16[2,512,768]{2,1,0:T(8,128)(2,1)} %wg.1, bf16[2,512,768]{2,1,0:T(8,128)(2,1)} %wu.1, bf16[2,768,512]{2,1,0:T(8,128)(2,1)} %wd.1), custom_call_target="tpu_custom_call" | custom-call | tf_op jit(solution)/shard_map/pallas_call | solution.py:333
  112.5 1.7 %copy.8 = bf16[64,2048]{1,0:T(8,128)(2,1)} copy(bf16[64,2048]{1,0:T(8,128)(2,1)} %shard_map.64) | data formatting | bytes 524288
